TPU v7x, 512 devices: a whole 4x8x8 slice. The times are simulated.
512 devices in a mesh: row: 8 (over y), col: 64 (over z, x, core).
Axes of the slice: x: 4, y: 8, z: 8, core: 2. Of those that a mesh axis runs over, the one named last changes fastest.
Arguments:
- sigma_top: bfloat16 [16384, 8, 64, 32], P('row', None, 'col'), as said below
- ancestor_rows: float32 [16384, 1024], P(('row', 'col')), may hold values from -0.0009765625 to 0.0009765625
- window_rows: float32 [1024, 1024], P('col'), may hold values from -0.1875 to 0.1875
- tile_inverse: float32 [4, 256, 256], replicated, as said below
- structure: int32 [4, 64], replicated, may hold values from 0 to 1, as said below
Outputs:
- cross_covariance: float32 [16384, 1024], P(('row', 'col'))
- window_covariance: float32 [1024, 1024], P('col')
Inputs may be any that keep to these rules, and one draw needn't show every extreme that they name: `sigma_top`: symmetric as an 16384 x 16384 matrix. `tile_inverse`: each tile is lower triangular. A tile in the structure of supernode j lies in the structure of every earlier supernode; supernode 0's structure holds every ancestor tile.
All inputs are finite; a program needn't handle non-finite values.
Results may differ from a plain program's by a relative error of at most 0.0013.
The roundings to bfloat16 on the way count: a program that leaves them out, or rounds other values in their place, can miss the bound.
Values may be sent and summed in bfloat16 or wider, within the bound.
No kernel may reach another device: no remote copies, remote signals or barrier semaphores. Data moves between devices by JAX's collectives and lax.ppermute only.
A program may use at most 64 MiB of HBM per device.

v0:
```python
import jax
import jax.numpy as jnp
from jax import lax
from jax.sharding import PartitionSpec as P


def lookup_rows(flags, tiles):
    matches = tiles[:, None] == jnp.arange(flags.shape[0], dtype=jnp.int32)[None, :]
    return jnp.sum(jnp.where(matches, flags[None, :], 0), axis=1).astype(jnp.float32)


def diagonal_total(partial_value):
    return lax.psum(partial_value, ("row", "col"))


def body(sigma_top, ancestor_rows, window_rows, tile_inverse, structure):
    highest = lax.Precision.HIGHEST
    supernodes = tile_inverse.shape[0]
    tile_width = tile_inverse.shape[1]
    window = supernodes * tile_width
    block_rows = sigma_top.shape[0]
    row_groups = sigma_top.shape[1]
    local_rows = ancestor_rows.shape[0]
    window_local = window_rows.shape[0]
    device_flat = lax.axis_index(("row", "col"))
    column_index = lax.axis_index("col")
    row_index = lax.axis_index("row")
    tiles_ancestor = (
        device_flat * local_rows + jnp.arange(local_rows, dtype=jnp.int32)
    ) // tile_width
    tiles_window = (
        column_index * window_local + jnp.arange(window_local, dtype=jnp.int32)
    ) // tile_width
    column_tiles = jnp.arange(window, dtype=jnp.int32) // tile_width
    upper_mask = column_tiles[None, :] > tiles_window[:, None]
    sigma_flat = sigma_top.reshape(block_rows, row_groups * local_rows)
    first_row = (row_index == 0).astype(jnp.float32)
    selections = [
        lookup_rows(structure[supernode], tiles_ancestor) for supernode in range(supernodes)
    ]
    cross = jnp.zeros((local_rows, window), jnp.float32)
    block = jnp.zeros((window_local, window), jnp.float32)
    for supernode in range(supernodes):
        left_edge = supernode * tile_width
        right_edge = left_edge + tile_width
        panel_product = jnp.dot(
            ancestor_rows[:, supernode * tile_width : (supernode + 1) * tile_width],
            tile_inverse[supernode],
            precision=highest,
            preferred_element_type=jnp.float32,
        )
        panel_anc = (selections[supernode][:, None] * panel_product).astype(jnp.bfloat16)
        keep = (tiles_window < supernode).astype(jnp.float32)
        product = jnp.dot(
            window_rows[:, supernode * tile_width : (supernode + 1) * tile_width],
            tile_inverse[supernode],
            precision=highest,
            preferred_element_type=jnp.float32,
        )
        panel_own = (keep[:, None] * product).astype(jnp.bfloat16)
        folded = lax.dot_general(
            sigma_flat,
            lax.all_gather(panel_anc, "col", axis=0, tiled=True),
            (((0,), (0,)), ((), ())),
            preferred_element_type=jnp.float32,
        )
        ancestor_part = lax.psum_scatter(
            folded.reshape(row_groups, local_rows, tile_width),
            "row",
            scatter_dimension=0,
            tiled=True,
        ).reshape(local_rows, tile_width)
        panel_all = lax.all_gather(panel_own, "col", axis=0, tiled=True)
        ancestor_f32 = panel_anc.astype(jnp.float32)
        own_f32 = panel_own.astype(jnp.float32)
        window_f32 = panel_all.astype(jnp.float32)
        result_ancestor = selections[supernode][:, None] * (
            ancestor_part
            + jnp.dot(cross, window_f32, precision=highest, preferred_element_type=jnp.float32)
        )
        diagonal_term = jnp.dot(
            ancestor_f32.T, result_ancestor, precision=highest, preferred_element_type=jnp.float32
        )
        if supernode > 0:
            upper = jnp.where(upper_mask, block, 0.0)
            upper_term = jnp.dot(
                upper, window_f32, precision=highest, preferred_element_type=jnp.float32
            )
            placed_term = lax.dynamic_update_slice_in_dim(
                jnp.zeros((window, tile_width), jnp.float32),
                upper_term,
                column_index * window_local,
                0,
            )
            window_term = jnp.dot(
                cross.T, ancestor_f32, precision=highest, preferred_element_type=jnp.float32
            )
            window_term = window_term + first_row * (
                jnp.dot(block.T, own_f32, precision=highest, preferred_element_type=jnp.float32)
                + placed_term
            )
            window_term = window_term[:left_edge]
            window_sum = lax.psum(window_term, ("row", "col"))
            diagonal_sum = diagonal_total(diagonal_term)
            result_window = jnp.concatenate(
                [window_sum, jnp.zeros((window - left_edge, tile_width), jnp.float32)], axis=0
            )
            window_part = jnp.dot(
                window_f32.T, result_window, precision=highest, preferred_element_type=jnp.float32
            )
            mine_result = lax.dynamic_slice_in_dim(
                result_window, column_index * window_local, window_local, 0
            )
        else:
            mine_result = jnp.zeros((window_local, tile_width), jnp.float32)
            window_part = jnp.zeros((tile_width, tile_width), jnp.float32)
            diagonal_sum = diagonal_total(diagonal_term)
        inverse = tile_inverse[supernode]
        diagonal = jnp.dot(
            inverse.T, inverse, precision=highest, preferred_element_type=jnp.float32
        )
        diagonal = diagonal + window_part + diagonal_sum
        placed = jnp.zeros((window, tile_width), jnp.float32).at[left_edge:right_edge].set(diagonal)
        mine_diagonal = lax.dynamic_slice_in_dim(
            placed, column_index * window_local, window_local, 0
        )
        row_tiles = tiles_window[:, None]
        column = jnp.where(
            row_tiles < supernode,
            -mine_result,
            jnp.where(row_tiles == supernode, mine_diagonal, 0.0),
        )
        cross = cross.at[:, left_edge:right_edge].set(-result_ancestor)
        block = block.at[:, left_edge:right_edge].set(column)
    return (cross, block)


def solution(mesh):
    placed = (P("row", None, "col", None), P(("row", "col"), None), P("col", None), P(), P())
    return jax.shard_map(
        body,
        mesh=mesh,
        in_specs=placed,
        out_specs=(P(("row", "col"), None), P("col", None)),
        check_vma=False,
    )
```

profile of v0, /device:TPU:23, one launch (start us, length us, event | category | flops | bytes accessed | tf_op | source)
XLA Modules:
  0.0 1614.0 jit_solution(3560617816976950300)
XLA Ops:
  8.2 1.8 fusion.22
  10.2 1.8 fusion.23
  12.1 1.8 fusion.24
  13.9 84.5 %all-gather.5.cloned.1.call-done = bf16[2048,256]{1,0:T(8,128)(2,1)} async-done(((bf16[32,256]{1,0:T(8,128)(2,1)}), bf16[2048,256]{1,0:T(8,128)(2,1)}) %all-gather.5.cloned.1.call-update) | async-done | bytes 1048592 | tf_op jit(solution)/shard_map/all_gather | solution.py:63
  98.5 2.5 fusion.111
  102.3 52.7 %all_gather.25 = bf16[1024,256]{1,0:T(8,128)(2,1)} all-gather(bf16[16,256]{1,0:T(8,128)(2,1)S(1)} %fusion.29), channel_id=1, replica_groups=mesh['row'=8,'col'=64] {'col'}, dimensions={0}, use_global_device_ids=true | all-gather | bytes 532480 | tf_op jit(solution)/shard_map/all_gather | solution.py:73
  155.3 49.1 %all_gather.27 = bf16[1024,256]{1,0:T(8,128)(2,1)S(1)} all-gather(bf16[16,256]{1,0:T(8,128)(2,1)S(1)} %fusion.30), channel_id=1, replica_groups=mesh['row'=8,'col'=64] {'col'}, dimensions={0}, use_global_device_ids=true | all-gather | bytes 532480 | tf_op jit(solution)/shard_map/all_gather | solution.py:73
  204.6 48.0 %all_gather.29 = bf16[1024,256]{1,0:T(8,128)(2,1)S(1)} all-gather(bf16[16,256]{1,0:T(8,128)(2,1)S(1)} %fusion.31), channel_id=1, replica_groups=mesh['row'=8,'col'=64] {'col'}, dimensions={0}, use_global_device_ids=true | all-gather | bytes 532480 | tf_op jit(solution)/shard_map/all_gather | solution.py:73
  252.8 54.0 %all_gather.31 = bf16[1024,256]{1,0:T(8,128)(2,1)} all-gather(bf16[16,256]{1,0:T(8,128)(2,1)S(1)} %fusion.32), channel_id=1, replica_groups=mesh['row'=8,'col'=64] {'col'}, dimensions={0}, use_global_device_ids=true | all-gather | bytes 532480 | tf_op jit(solution)/shard_map/all_gather | solution.py:73
  306.9 1.3 fusion.41
  308.2 2.4 fusion.112
  312.0 2.4 fusion.113
  316.4 2.1 negate_select_fusion
  319.6 70.1 %all-gather.11.cloned.1.call-done = bf16[2048,256]{1,0:T(8,128)(2,1)} async-done(((bf16[32,256]{1,0:T(8,128)(2,1)}), bf16[2048,256]{1,0:T(8,128)(2,1)}) %all-gather.11.cloned.1.call-update) | async-done | bytes 1048592 | tf_op jit(solution)/shard_map/all_gather | solution.py:63
  389.7 2.4 fusion.114
  392.8 1.6 fusion.60
  394.4 28.6 %reduce-scatter.7.cloned.1.call-done = f32[1,32,256]{2,1,0:T(8,128)} async-done(((f32[8,32,256]{2,1,0:T(8,128)}), f32[1,32,256]{2,1,0:T(8,128)}) %reduce-scatter.7.cloned.1.call-update) | async-done | bytes 32784 | tf_op jit(solution)/shard_map/reduce_scatter | solution.py:67
  422.9 1.7 select_dynamic-update-slice_fusion
  425.7 1.6 fusion.105
  427.3 36.5 %reduce-scatter.9.cloned.1.call-done = f32[1,32,256]{2,1,0:T(8,128)} async-done(((f32[8,32,256]{2,1,0:T(8,128)}), f32[1,32,256]{2,1,0:T(8,128)}) %reduce-scatter.9.cloned.1.call-update) | async-done | bytes 32784 | tf_op jit(solution)/shard_map/reduce_scatter | solution.py:67
  466.0 277.6 %all-reduce.17.cloned.1.call-done = f32[256,256]{1,0:T(8,128)} async-done(((f32[256,256]{1,0:T(8,128)}), f32[256,256]{1,0:T(8,128)}) %all-reduce.17.cloned.1.call-update) | async-done | bytes 262160 | tf_op jit(solution)/shard_map/psum | solution.py:13
  743.6 1.5 convolution_add_fusion.1
  746.8 1.7 slice_add_fusion.2
  749.2 25.0 %reduce-scatter.11.cloned.1.call-done = f32[1,32,256]{2,1,0:T(8,128)} async-done(((f32[8,32,256]{2,1,0:T(8,128)}), f32[1,32,256]{2,1,0:T(8,128)}) %reduce-scatter.11.cloned.1.call-update) | async-done | bytes 32784 | tf_op jit(solution)/shard_map/reduce_scatter | solution.py:67
  774.2 1.4 fusion.18
  775.6 281.1 %all-reduce.23.cloned.1.call-done = (f32[256,256]{1,0:T(8,128)}, f32[256,256]{1,0:T(8,128)}) async-done(((f32[256,256]{1,0:T(8,128)}, f32[256,256]{1,0:T(8,128)}), (f32[256,256]{1,0:T(8,128)}, f32[256,256]{1,0:T(8,128)})) %all-reduce.23.cloned.1.call-update) | async-done | bytes 524304 | tf_op jit(solution)/shard_map/psum | solution.py:13
  1056.7 1.8 fusion.13
  1063.0 1.6 fusion.108
  1064.6 265.4 %all-reduce.21.cloned.1.call-done = (f32[256,256]{1,0:T(8,128)}, f32[512,256]{1,0:T(8,128)}) async-done(((f32[256,256]{1,0:T(8,128)}, f32[512,256]{1,0:T(8,128)}), (f32[256,256]{1,0:T(8,128)}, f32[512,256]{1,0:T(8,128)})) %all-reduce.21.cloned.1.call-update) | async-done | bytes 786448 | tf_op jit(solution)/shard_map/psum | solution.py:13
  1330.0 2.0 fusion.7
  1335.8 268.6 %all-reduce.19.cloned.1.call-done = (f32[256,256]{1,0:T(8,128)}, f32[768,256]{1,0:T(8,128)}) async-done(((f32[256,256]{1,0:T(8,128)}, f32[768,256]{1,0:T(8,128)}), (f32[256,256]{1,0:T(8,128)}, f32[768,256]{1,0:T(8,128)})) %all-reduce.19.cloned.1.call-update) | async-done | bytes 1048592 | tf_op jit(solution)/shard_map/psum | solution.py:13
  1604.4 2.0 fusion.16
  (109 shorter events, 22.7 us)
Async XLA Ops:
  7.2 91.3 %copy-start = (bf16[2048,8,1,32]{0,3,2,1:T(8,128)(2,1)S(1)}, bf16[2048,8,1,32]{0,3,2,1:T(8,128)(2,1)}, u32[]{:S(2)}) copy-start(bf16[2048,8,1,32]{0,3,2,1:T(8,128)(2,1)} %param.29) | copy-start | bytes 3145732
  7.2 91.3 %all-gather.5.cloned.1.call-start = ((), (), s32[]{:S(2)}) async-start(), calls=%async_computation.4 | async-start | bytes 1064960 | tf_op jit(solution)/shard_map/all_gather | solution.py:63
  7.2 0.8 copy-start.16
  8.2 1.9 copy-start.14
  10.1 298.1 %all-gather.7.cloned.1.call-start = ((), (), s32[]{:S(2)}) async-start(), calls=%async_computation.6 | async-start | bytes 1064960 | tf_op jit(solution)/shard_map/all_gather | solution.py:63
  12.0 300.0 %all-gather.9.cloned.1.call-start = ((), (), s32[]{:S(2)}) async-start(), calls=%async_computation.8 | async-start | bytes 1064960 | tf_op jit(solution)/shard_map/all_gather | solution.py:63
  13.9 302.6 %reduce-scatter.5.cloned.1.call-start = ((), (), s32[]{:S(2)}) async-start(), calls=%async_computation.5 | async-start | bytes 294912 | tf_op jit(solution)/shard_map/reduce_scatter | solution.py:67
  98.5 2.6 copy-start.1
  101.0 288.7 %all-gather.11.cloned.1.call-start = ((), (), s32[]{:S(2)}) async-start(), calls=%async_computation.10 | async-start | bytes 1064960 | tf_op jit(solution)/shard_map/all_gather | solution.py:63
  101.0 1.0 copy-start.15
  101.9 321.0 %reduce-scatter.7.cloned.1.call-start = ((), (), s32[]{:S(2)}) async-start(), calls=%async_computation.7 | async-start | bytes 294912 | tf_op jit(solution)/shard_map/reduce_scatter | solution.py:67
  310.6 153.2 %reduce-scatter.9.cloned.1.call-start = ((), (), s32[]{:S(2)}) async-start(), calls=%async_computation.9 | async-start | bytes 294912 | tf_op jit(solution)/shard_map/reduce_scatter | solution.py:67
  314.4 429.2 %all-reduce.17.cloned.1.call-start = ((), (), s32[]{:S(2)}) async-start(), calls=%async_computation.12 | async-start | bytes 524288 | tf_op jit(solution)/shard_map/psum | solution.py:13
  316.4 2.1 copy-start.13
  319.6 454.6 %reduce-scatter.11.cloned.1.call-start = ((), (), s32[]{:S(2)}) async-start(), calls=%async_computation.11 | async-start | bytes 294912 | tf_op jit(solution)/shard_map/reduce_scatter | solution.py:67
  392.0 0.7 copy-start.11
  392.1 664.6 %all-reduce.23.cloned.1.call-start = ((), (), s32[]{:S(2)}) async-start(), calls=%async_computation.15 | async-start | bytes 1048576 | tf_op jit(solution)/shard_map/psum | solution.py:13
  424.7 1.1 copy-start.12
  748.5 581.4 %all-reduce.21.cloned.1.call-start = ((), (), s32[]{:S(2)}) async-start(), calls=%async_computation.14 | async-start | bytes 1572864 | tf_op jit(solution)/shard_map/psum | solution.py:13
  1056.7 1.8 copy-start.9
  1058.5 1.8 copy-start.6
  1061.2 0.7 copy-start.10
  1061.3 543.2 %all-reduce.19.cloned.1.call-start = ((), (), s32[]{:S(2)}) async-start(), calls=%async_computation.13 | async-start | bytes 2097152 | tf_op jit(solution)/shard_map/psum | solution.py:13
  1330.0 2.0 copy-start.7
  1332.7 1.0 copy-start.2
  1332.7 1.4 copy-start.4
  1335.8 270.7 %copy-start.3 = (f32[32,1024]{1,0:T(8,128)}, f32[32,1024]{1,0:T(8,128)S(1)}, u32[]{:S(2)}) copy-start(f32[32,1024]{1,0:T(8,128)S(1)} %negate_dynamic-update-slice_fusion) | copy-start | bytes 393220
  1604.4 2.0 copy-start.5
  1606.5 0.6 copy-start.8
Sparse Core Ops, SparseCore 0:
  11.9 86.4 all-gather.4
  102.4 79.7 all-gather.6
  185.5 79.7 all-gather.8
  268.0 30.7 reduce-scatter.4
  302.6 87.0 all-gather.10
  392.5 30.3 reduce-scatter.6
  425.7 38.0 reduce-scatter.8
  469.6 273.9 all-reduce.16
  746.4 27.7 reduce-scatter.10
  780.1 276.5 all-reduce.22
  1061.9 268.0 all-reduce.20
  1335.3 269.0 all-reduce.18
where the time goes:
time: 1610 us
  waiting for transfers between devices  1340 us (83%)
  blocking collectives  204 us (13%)
  matrix products  45.4 us (3%)
    psum x4, waiting for transfers between devices, diagonal_total(): return lax.psum(partial_value, ('row', 'col'))  1090 us
    all_gather x4, blocking collectives, body(): panel_all = lax.all_gather(panel_own, 'col', axis=0, tiled=True)  204 us
    all_gather x4, waiting for transfers between devices, body(): lax.all_gather(panel_anc, 'col', axis=0, tiled=True)  155 us
    reduce_scatter x4, waiting for transfers between devices, body(): lax.psum_scatter(folded.reshape(row_groups, local_rows, tile_width), 'row...  90 us
  transfers between devices with their start and end apart: 12, of which 9 were waited for; matrix products, arithmetic and copies ran while one was open for 3% of the time, Pallas kernels for 0%

commit v1 on v0

--- a/solution.py
+++ b/solution.py
@@ -1,7 +1,17 @@
+import functools
 import jax
 import jax.numpy as jnp
 from jax import lax
 from jax.sharding import PartitionSpec as P
+
+
+def refer_corner(xin, chip_axis):
+    return lax.all_to_all(
+        jnp.concatenate(lax.axis_size(chip_axis) * [xin], axis=0), chip_axis, 0, 0, tiled=True
+    )
+
+
+_manage_quotas = functools.partial(refer_corner, chip_axis="col")
 
 
 def lookup_rows(flags, tiles):
@@ -60,7 +70,7 @@
         panel_own = (keep[:, None] * product).astype(jnp.bfloat16)
         folded = lax.dot_general(
             sigma_flat,
-            lax.all_gather(panel_anc, "col", axis=0, tiled=True),
+            _manage_quotas(panel_anc),
             (((0,), (0,)), ((), ())),
             preferred_element_type=jnp.float32,
         )

time: 1610 us -> 1600 us (level)
  waiting for transfers between devices: 1340 us -> 1230 us
  starting transfers between devices: 0.72 us -> 42.2 us
  local copies, waits for them, and re-layouts: 2.93 us -> 42.4 us
    all_gather x4 -> x0, waiting for transfers between devices: 155 us -> none  [body(): lax.all_gather(panel_anc, 'col', axis=0, tiled=True)]
    all_to_all x0 -> x4, starting transfers between devices: none -> 41.7 us  [refer_corner(): lax.all_to_all(jnp.concatenate(lax.axis_size(chip_axis) * [xin], axis=0),...]
    unnamed x34 -> x282, local copies, waits for them, and re-layouts: 2.91 us -> 41.7 us
    reduce_scatter x4, waiting for transfers between devices: 90 us -> 120 us  [body(): lax.psum_scatter(folded.reshape(row_groups, local_rows, tile_width), 'row...]
  transfers between devices with their start and end apart: 12 -> 12, of which waited for: 9 -> 9; matrix products, arithmetic and copies ran while one was open for 3% -> 5% of each run, Pallas kernels for 0% -> 0%
where the time goes in v1:
time: 1600 us
  waiting for transfers between devices  1230 us (77%)
  blocking collectives  219 us (14%)
  local copies, waits for them, and re-layouts  42.4 us (3%)
  starting transfers between devices  42.2 us (3%)
  matrix products  41.6 us (3%)
  between operations  16.1 us (1%)
    psum x4, waiting for transfers between devices, diagonal_total(): return lax.psum(partial_value, ('row', 'col'))  1090 us
    all_gather x4, blocking collectives, body(): panel_all = lax.all_gather(panel_own, 'col', axis=0, tiled=True)  219 us
    reduce_scatter x4, waiting for transfers between devices, body(): lax.psum_scatter(folded.reshape(row_groups, local_rows, tile_width), 'row...  120 us
    unnamed x282, local copies, waits for them, and re-layouts  41.7 us
    all_to_all x4, starting transfers between devices, refer_corner(): lax.all_to_all(jnp.concatenate(lax.axis_size(chip_axis) * [xin], axis=0),...  41.7 us
  transfers between devices with their start and end apart: 12, of which 9 were waited for; matrix products, arithmetic and copies ran while one was open for 5% of the time, Pallas kernels for 0%

profile of v1, /device:TPU:23, one launch (start us, length us, event | category | flops | bytes accessed | tf_op | source)
XLA Modules:
  0.0 1599.6 jit_solution(14770461197538024939)
XLA Ops:
  11.1 14.3 all-to-all-start
  53.4 10.5 all-to-all-start.1
  74.7 16.1 %all-to-all-done.1 = bf16[64,32,256]{2,1,0:T(8,128)(2,1)} async-done(((bf16[64,32,256]{2,1,0:T(8,128)(2,1)}), bf16[64,32,256]{2,1,0:T(8,128)(2,1)}, u32[]{:S(2)}, u32[]{:S(2)}) %all-to-all-start.1) | async-done | bytes 1048608 | tf_op jit(solution)/shard_map/all_to_all | solution.py:9
  90.8 7.6 all-to-all-start.2
  101.7 69.1 %all_gather.12 = bf16[1024,256]{1,0:T(8,128)(2,1)} all-gather(bf16[16,256]{1,0:T(8,128)(2,1)S(1)} %fusion.29), channel_id=1, replica_groups=mesh['row'=8,'col'=64] {'col'}, dimensions={0}, use_global_device_ids=true | all-gather | bytes 532480 | tf_op jit(solution)/shard_map/all_gather | solution.py:83
  171.1 48.0 %all_gather.13 = bf16[1024,256]{1,0:T(8,128)(2,1)S(1)} all-gather(bf16[16,256]{1,0:T(8,128)(2,1)S(1)} %fusion.30), channel_id=1, replica_groups=mesh['row'=8,'col'=64] {'col'}, dimensions={0}, use_global_device_ids=true | all-gather | bytes 532480 | tf_op jit(solution)/shard_map/all_gather | solution.py:83
  219.3 49.4 %all_gather.14 = bf16[1024,256]{1,0:T(8,128)(2,1)S(1)} all-gather(bf16[16,256]{1,0:T(8,128)(2,1)S(1)} %fusion.31), channel_id=1, replica_groups=mesh['row'=8,'col'=64] {'col'}, dimensions={0}, use_global_device_ids=true | all-gather | bytes 532480 | tf_op jit(solution)/shard_map/all_gather | solution.py:83
  268.9 52.5 %all_gather.15 = bf16[1024,256]{1,0:T(8,128)(2,1)} all-gather(bf16[16,256]{1,0:T(8,128)(2,1)S(1)} %fusion.32), channel_id=1, replica_groups=mesh['row'=8,'col'=64] {'col'}, dimensions={0}, use_global_device_ids=true | all-gather | bytes 532480 | tf_op jit(solution)/shard_map/all_gather | solution.py:83
  321.5 9.3 all-to-all-start.3
  330.8 2.4 fusion.111
  334.6 2.4 fusion.112
  338.4 2.4 fusion.113
  342.8 26.1 %reduce-scatter.5.cloned.1.call-done = f32[1,32,256]{2,1,0:T(8,128)} async-done(((f32[8,32,256]{2,1,0:T(8,128)}), f32[1,32,256]{2,1,0:T(8,128)}) %reduce-scatter.5.cloned.1.call-update) | async-done | bytes 32784 | tf_op jit(solution)/shard_map/reduce_scatter | solution.py:77
  368.8 2.1 negate_select_fusion
  372.0 2.4 fusion.114
  374.7 1.6 fusion.60
  376.3 32.6 %reduce-scatter.7.cloned.1.call-done = f32[1,32,256]{2,1,0:T(8,128)} async-done(((f32[8,32,256]{2,1,0:T(8,128)}), f32[1,32,256]{2,1,0:T(8,128)}) %reduce-scatter.7.cloned.1.call-update) | async-done | bytes 32784 | tf_op jit(solution)/shard_map/reduce_scatter | solution.py:77
  408.9 1.8 select_dynamic-update-slice_fusion
  411.7 1.6 fusion.105
  413.3 36.6 %reduce-scatter.9.cloned.1.call-done = f32[1,32,256]{2,1,0:T(8,128)} async-done(((f32[8,32,256]{2,1,0:T(8,128)}), f32[1,32,256]{2,1,0:T(8,128)}) %reduce-scatter.9.cloned.1.call-update) | async-done | bytes 32784 | tf_op jit(solution)/shard_map/reduce_scatter | solution.py:77
  452.0 277.5 %all-reduce.17.cloned.1.call-done = f32[256,256]{1,0:T(8,128)} async-done(((f32[256,256]{1,0:T(8,128)}), f32[256,256]{1,0:T(8,128)}) %all-reduce.17.cloned.1.call-update) | async-done | bytes 262160 | tf_op jit(solution)/shard_map/psum | solution.py:23
  729.5 1.5 convolution_add_fusion.1
  732.7 1.7 slice_add_fusion.2
  735.1 24.8 %reduce-scatter.11.cloned.1.call-done = f32[1,32,256]{2,1,0:T(8,128)} async-done(((f32[8,32,256]{2,1,0:T(8,128)}), f32[1,32,256]{2,1,0:T(8,128)}) %reduce-scatter.11.cloned.1.call-update) | async-done | bytes 32784 | tf_op jit(solution)/shard_map/reduce_scatter | solution.py:77
  760.0 1.4 fusion.18
  761.4 281.0 %all-reduce.23.cloned.1.call-done = (f32[256,256]{1,0:T(8,128)}, f32[256,256]{1,0:T(8,128)}) async-done(((f32[256,256]{1,0:T(8,128)}, f32[256,256]{1,0:T(8,128)}), (f32[256,256]{1,0:T(8,128)}, f32[256,256]{1,0:T(8,128)})) %all-reduce.23.cloned.1.call-update) | async-done | bytes 524304 | tf_op jit(solution)/shard_map/psum | solution.py:23
  1042.4 1.8 fusion.13
  1048.0 1.6 fusion.108
  1049.7 266.0 %all-reduce.21.cloned.1.call-done = (f32[256,256]{1,0:T(8,128)}, f32[512,256]{1,0:T(8,128)}) async-done(((f32[256,256]{1,0:T(8,128)}, f32[512,256]{1,0:T(8,128)}), (f32[256,256]{1,0:T(8,128)}, f32[512,256]{1,0:T(8,128)})) %all-reduce.21.cloned.1.call-update) | async-done | bytes 786448 | tf_op jit(solution)/shard_map/psum | solution.py:23
  1315.6 2.0 fusion.7
  1321.5 268.6 %all-reduce.19.cloned.1.call-done = (f32[256,256]{1,0:T(8,128)}, f32[768,256]{1,0:T(8,128)}) async-done(((f32[256,256]{1,0:T(8,128)}, f32[768,256]{1,0:T(8,128)}), (f32[256,256]{1,0:T(8,128)}, f32[768,256]{1,0:T(8,128)})) %all-reduce.19.cloned.1.call-update) | async-done | bytes 1048592 | tf_op jit(solution)/shard_map/psum | solution.py:23
  1590.0 2.0 fusion.16
  (357 shorter events, 64.9 us)
Async XLA Ops:
  7.2 323.7 %copy-start = (bf16[2048,8,1,32]{0,3,2,1:T(8,128)(2,1)S(1)}, bf16[2048,8,1,32]{0,3,2,1:T(8,128)(2,1)}, u32[]{:S(2)}) copy-start(bf16[2048,8,1,32]{0,3,2,1:T(8,128)(2,1)} %param.29) | copy-start | bytes 3145732
  7.2 0.8 copy-start.16
  10.1 1.0 copy-start.10
  11.1 14.3 copy-start.1
  11.1 14.3 copy-start.14
  11.1 41.3 %all-to-all-start = ((bf16[64,32,256]{2,1,0:T(8,128)(2,1)}), bf16[64,32,256]{2,1,0:T(8,128)(2,1)S(1)}, u32[]{:S(2)}, u32[]{:S(2)}) async-start(bf16[64,32,256]{2,1,0:T(8,128)(2,1)} %bitcast.116), calls=%async_computation | async-start | bytes 2097152 | tf_op jit(solution)/shard_map/all_to_all | solution.py:9
  26.4 1.0 copy-start.11
  27.5 24.4 %copy-start.12 = (bf16[2048,256]{1,0:T(8,128)(2,1)}, bf16[2048,256]{1,0:T(8,128)(2,1)S(1)}, u32[]{:S(2)}) copy-start(bf16[2048,256]{1,0:T(8,128)(2,1)S(1)} %constant_dynamic-update-slice_fusion.128) | copy-start | bytes 3145732
  52.5 1.0 copy-start.3
  53.4 37.4 %all-to-all-start.1 = ((bf16[64,32,256]{2,1,0:T(8,128)(2,1)}), bf16[64,32,256]{2,1,0:T(8,128)(2,1)}, u32[]{:S(2)}, u32[]{:S(2)}) async-start(bf16[64,32,256]{2,1,0:T(8,128)(2,1)} %bitcast.117), calls=%async_computation.2 | async-start | bytes 2097152 | tf_op jit(solution)/shard_map/all_to_all | solution.py:9
  90.8 230.6 %all-to-all-start.2 = ((bf16[64,32,256]{2,1,0:T(8,128)(2,1)}), bf16[64,32,256]{2,1,0:T(8,128)(2,1)}, u32[]{:S(2)}, u32[]{:S(2)}) async-start(bf16[64,32,256]{2,1,0:T(8,128)(2,1)} %bitcast.118), calls=%async_computation.4 | async-start | bytes 2097152 | tf_op jit(solution)/shard_map/all_to_all | solution.py:9
  99.1 2.4 copy-start.15
  321.5 50.5 %all-to-all-start.3 = ((bf16[64,32,256]{2,1,0:T(8,128)(2,1)}), bf16[64,32,256]{2,1,0:T(8,128)(2,1)}, u32[]{:S(2)}, u32[]{:S(2)}) async-start(bf16[64,32,256]{2,1,0:T(8,128)(2,1)} %bitcast.24), calls=%async_computation.6 | async-start | bytes 2097152 | tf_op jit(solution)/shard_map/all_to_all | solution.py:9
  330.8 38.0 %reduce-scatter.5.cloned.1.call-start = ((), (), s32[]{:S(2)}) async-start(), calls=%async_computation.8 | async-start | bytes 294912 | tf_op jit(solution)/shard_map/reduce_scatter | solution.py:77
  333.2 75.6 %reduce-scatter.7.cloned.1.call-start = ((), (), s32[]{:S(2)}) async-start(), calls=%async_computation.9 | async-start | bytes 294912 | tf_op jit(solution)/shard_map/reduce_scatter | solution.py:77
  337.0 112.9 %reduce-scatter.9.cloned.1.call-start = ((), (), s32[]{:S(2)}) async-start(), calls=%async_computation.10 | async-start | bytes 294912 | tf_op jit(solution)/shard_map/reduce_scatter | solution.py:77
  340.7 388.8 %all-reduce.17.cloned.1.call-start = ((), (), s32[]{:S(2)}) async-start(), calls=%async_computation.12 | async-start | bytes 524288 | tf_op jit(solution)/shard_map/psum | solution.py:23
  371.9 388.0 %reduce-scatter.11.cloned.1.call-start = ((), (), s32[]{:S(2)}) async-start(), calls=%async_computation.11 | async-start | bytes 294912 | tf_op jit(solution)/shard_map/reduce_scatter | solution.py:77
  374.4 668.0 %all-reduce.23.cloned.1.call-start = ((), (), s32[]{:S(2)}) async-start(), calls=%async_computation.15 | async-start | bytes 1048576 | tf_op jit(solution)/shard_map/psum | solution.py:23
  734.5 581.2 %all-reduce.21.cloned.1.call-start = ((), (), s32[]{:S(2)}) async-start(), calls=%async_computation.14 | async-start | bytes 1572864 | tf_op jit(solution)/shard_map/psum | solution.py:23
  1042.4 1.8 copy-start.13
  1044.2 1.8 copy-start.7
  1046.9 543.1 %all-reduce.19.cloned.1.call-start = ((), (), s32[]{:S(2)}) async-start(), calls=%async_computation.13 | async-start | bytes 2097152 | tf_op jit(solution)/shard_map/psum | solution.py:23
  1315.6 2.0 copy-start.8
  1318.4 1.0 copy-start.2
  1318.4 1.4 copy-start.5
  1321.4 270.6 %copy-start.4 = (f32[32,1024]{1,0:T(8,128)}, f32[32,1024]{1,0:T(8,128)S(1)}, u32[]{:S(2)}) copy-start(f32[32,1024]{1,0:T(8,128)S(1)} %negate_dynamic-update-slice_fusion) | copy-start | bytes 393220
  1590.0 2.0 copy-start.6
  1592.2 0.6 copy-start.9
Sparse Core Ops, SparseCore 0:
  334.4 34.3 reduce-scatter.4
  371.8 37.0 reduce-scatter.6
  411.7 38.1 reduce-scatter.8
  455.5 273.9 all-reduce.16
  732.1 27.7 reduce-scatter.10
  765.8 276.4 all-reduce.22
  1047.5 268.0 all-reduce.20
  1320.9 269.0 all-reduce.18
